TPU v7x, 32 devices: a whole 2x2x4 slice. The times are simulated.
32 devices in a mesh: row: 4 (over y, x), col: 8 (over z, core).
Axes of the slice: x: 2, y: 2, z: 4, core: 2. Of those that a mesh axis runs over, the one named last changes fastest.
Arguments:
- tiles: bfloat16 [256, 256, 256], P(('row', 'col')), may hold values from -0.09375 to 0.09375
- tile_rows: int32 [256], P(('row', 'col')), may hold values from 0 to 3, as said below
- tile_cols: int32 [256], P(('row', 'col')), may hold values from 0 to 1
- tile_count: int32 [32], P(('row', 'col')), may hold values from 0 to 8, as said below
- bounds: float32 [2], replicated, may hold values from -1 to 2, as said below
- vectors: float32 [4096, 128], P(('row', 'col')), may hold values from -6 to 6
Outputs:
- filtered: float32 [4096, 128], P(('row', 'col'))
- gram: float32 [128, 128], replicated
Inputs may be any that keep to these rules, and one draw needn't show every extreme that they name: `tile_rows`: within each device the first tile_count slots name distinct blocks with global block row I <= global block column J; the device's diagonal blocks (I = J) come first; every diagonal block of the Hamiltonian is stored; slots after the live ones hold valid indices but are not part of the matrix. `tile_count`: devices whose block rows all lie below their block columns have no live slot; some device has all 8 slots live. bounds[0] < -0.5 and bounds[1] > 1.0.
All inputs are finite; a program needn't handle non-finite values.
Results may differ from a plain program's by a relative error of at most 0.0037.
Values may be sent and summed in bfloat16 or wider, within the bound.
A program may use at most 64 MiB of HBM per device.

v0:
```python
import jax
import jax.numpy as jnp
from jax import lax
from jax.sharding import PartitionSpec as P

BLK_COL = 2


def spread(block, axis, holder):
    block = jnp.where(lax.axis_index(axis) == holder, block, jnp.zeros_like(block))
    return lax.psum(block, axis)


def on_device(tiles, tile_rows, tile_cols, tile_count, bounds, vectors):
    col_ratio = lax.axis_size("col") // lax.axis_size("row")
    col_index = lax.axis_index("col")
    row_index = lax.axis_index("row")
    root_row = col_index // col_ratio
    slot_total = tiles.shape[0]
    block_size = tiles.shape[1]
    share_rows = vectors.shape[0]
    width_vecs = vectors.shape[1]
    group_rows = share_rows * lax.axis_size("col")
    group_blocks = group_rows // block_size
    column_rows = BLK_COL * block_size
    total_rows = share_rows * lax.axis_size("row") * lax.axis_size("col")
    offset = col_index % col_ratio * column_rows
    live_mask = (jnp.arange(slot_total, dtype=jnp.int32) < tile_count[0]).astype(jnp.bfloat16)
    owner_flag = (row_index == root_row).astype(jnp.float32)
    center = (bounds[1] + bounds[0]) * 0.5
    halfwidth = (bounds[1] - bounds[0]) * 0.5

    def apply_hamiltonian(current_vec):
        vector_panel = current_vec.astype(jnp.bfloat16)
        row_panel = lax.all_gather(vector_panel, "col", axis=0, tiled=True)
        col_piece = lax.dynamic_slice_in_dim(row_panel, offset, column_rows, 0)
        col_panel = spread(col_piece, "row", root_row)
        row_input = row_panel.reshape(group_blocks, block_size, width_vecs)
        col_input = col_panel.reshape(BLK_COL, block_size, width_vecs)
        start_rows = jnp.zeros((group_blocks, block_size, width_vecs), jnp.float32)
        start_cols = jnp.zeros((BLK_COL, block_size, width_vecs), jnp.float32)
        masked_cols = col_input[tile_cols] * live_mask[:, None, None]
        masked_rows = row_input[tile_rows] * live_mask[:, None, None]
        forward = jnp.einsum("tab,tbk->tak", tiles, masked_cols, preferred_element_type=jnp.float32)
        backward = jnp.einsum(
            "tab,tak->tbk", tiles, masked_rows, preferred_element_type=jnp.float32
        )
        row_part = start_rows.at[tile_rows].add(forward)
        col_part = start_cols.at[tile_cols].add(backward)
        column_total = lax.psum(col_part, "row")
        row_part = row_part.reshape(group_rows, width_vecs)
        present = lax.dynamic_slice_in_dim(row_part, offset, column_rows, 0)
        updated = present + owner_flag * column_total.reshape(column_rows, width_vecs)
        row_part = lax.dynamic_update_slice_in_dim(row_part, updated, offset, 0)
        return lax.psum_scatter(row_part, "col", scatter_dimension=0, tiled=True)

    current_vec = (apply_hamiltonian(vectors) - center * vectors) / halfwidth
    image = apply_hamiltonian(current_vec)
    following = 2.0 * (image - center * current_vec) / halfwidth - vectors
    current_vec = following
    gram_local = lax.dot_general(
        current_vec,
        current_vec,
        (((0,), (0,)), ((), ())),
        precision=lax.Precision.HIGHEST,
        preferred_element_type=jnp.float32,
    )
    gram_total = lax.psum(gram_local, ("row", "col"))
    return (current_vec, gram_total / total_rows)


def solution(mesh):
    in_specs = (
        P(("row", "col"), None, None),
        P(("row", "col")),
        P(("row", "col")),
        P(("row", "col")),
        P(),
        P(("row", "col"), None),
    )
    out_specs = (P(("row", "col"), None), P())
    return jax.shard_map(
        on_device, mesh=mesh, in_specs=in_specs, out_specs=out_specs, check_vma=False
    )
```

profile of v0, /device:TPU:1, one launch (start us, length us, event | category | flops | bytes accessed | tf_op | source)
XLA Modules:
  0.0 414.4 jit_solution(1064199134010569408)
XLA Ops:
  7.2 0.9 convert_element_type.16
  8.2 15.8 %all_gather.6 = bf16[1024,128]{1,0:T(8,128)(2,1)S(1)} all-gather(bf16[128,128]{1,0:T(8,128)(2,1)S(1)} %convert_element_type.16), channel_id=1, replica_groups=mesh['row'=4,'col'=8] {'col'}, dimensions={0}, use_global_device_ids=true | all-gather | bytes 294912 | tf_op jit(solution)/shard_map/all_gather | solution.py:35
  23.9 0.7 dynamic-slice_select_fusion.1
  27.8 1.3 scatter_fusion.1
  29.1 0.7 copy-done.4
  29.9 37.0 %all-reduce.6.cloned.1.call-done = bf16[2,256,128]{2,1,0:T(8,128)(2,1)} async-done(((bf16[2,256,128]{2,1,0:T(8,128)(2,1)}), bf16[2,256,128]{2,1,0:T(8,128)(2,1)}) %all-reduce.6.cloned.1.call-update) | async-done | bytes 131088 | tf_op jit(solution)/shard_map/psum | solution.py:11
  66.9 1.5 gather_fusion
  68.5 1.7 convolution_bitcast_fusion.3
  70.2 1.5 copy.13
  71.8 1.3 scatter_fusion
  73.1 39.9 %all-reduce.8.cloned.1.call-done = f32[2,256,128]{2,1,0:T(8,128)} async-done(((f32[2,256,128]{2,1,0:T(8,128)}), f32[2,256,128]{2,1,0:T(8,128)}) %all-reduce.8.cloned.1.call-update) | async-done | bytes 262160 | tf_op jit(solution)/shard_map/psum | solution.py:50
  113.1 1.0 broadcast_multiply_fusion.1
  114.1 0.8 copy-done.2
  118.1 25.2 %reduce-scatter.3.cloned.1.call-done = f32[128,128]{1,0:T(8,128)} async-done(((f32[1024,128]{1,0:T(8,128)}), f32[128,128]{1,0:T(8,128)}) %reduce-scatter.3.cloned.1.call-update) | async-done | bytes 65552 | tf_op jit(solution)/shard_map/reduce_scatter | solution.py:55
  143.4 0.9 fusion.8
  144.2 18.0 %all_gather.7 = bf16[1024,128]{1,0:T(8,128)(2,1)S(1)} all-gather(bf16[128,128]{1,0:T(8,128)(2,1)S(1)} %fusion.8), channel_id=1, replica_groups=mesh['row'=4,'col'=8] {'col'}, dimensions={0}, use_global_device_ids=true | all-gather | bytes 294912 | tf_op jit(solution)/shard_map/all_gather | solution.py:35
  162.3 0.7 dynamic-slice_select_fusion
  164.4 1.3 scatter_fusion.3
  165.8 0.7 copy-done.3
  166.6 36.5 %all-reduce.10.cloned.1.call-done = bf16[2,256,128]{2,1,0:T(8,128)(2,1)} async-done(((bf16[2,256,128]{2,1,0:T(8,128)(2,1)}), bf16[2,256,128]{2,1,0:T(8,128)(2,1)}) %all-reduce.10.cloned.1.call-update) | async-done | bytes 131088 | tf_op jit(solution)/shard_map/psum | solution.py:11
  203.1 1.5 gather_fusion.2
  204.7 1.7 convolution_bitcast_fusion.1
  206.4 1.5 copy.17
  208.0 1.3 scatter_fusion.2
  209.3 39.5 %all-reduce.12.cloned.1.call-done = f32[2,256,128]{2,1,0:T(8,128)} async-done(((f32[2,256,128]{2,1,0:T(8,128)}), f32[2,256,128]{2,1,0:T(8,128)}) %all-reduce.12.cloned.1.call-update) | async-done | bytes 262160 | tf_op jit(solution)/shard_map/psum | solution.py:50
  248.8 1.0 broadcast_multiply_fusion
  249.9 0.8 copy-done.1
  250.7 28.2 %reduce-scatter.5.cloned.1.call-done = f32[128,128]{1,0:T(8,128)} async-done(((f32[1024,128]{1,0:T(8,128)}), f32[128,128]{1,0:T(8,128)}) %reduce-scatter.5.cloned.1.call-update) | async-done | bytes 65552 | tf_op jit(solution)/shard_map/reduce_scatter | solution.py:55
  278.9 0.9 divide_subtract_fusion
  279.8 0.9 fusion.10
  280.8 125.3 %all-reduce.14.cloned.1.call-done = f32[128,128]{1,0:T(8,128)} async-done(((f32[128,128]{1,0:T(8,128)}), f32[128,128]{1,0:T(8,128)}) %all-reduce.14.cloned.1.call-update) | async-done | bytes 65552 | tf_op jit(solution)/shard_map/psum | solution.py:68
  406.1 1.5 broadcast_multiply_fusion.2
  (50 shorter events, 5.0 us)
Async XLA Ops:
  7.2 19.5 %copy-start = (bf16[8,256,256]{2,1,0:T(8,128)(2,1)S(1)}, bf16[8,256,256]{2,1,0:T(8,128)(2,1)}, u32[]{:S(2)}) copy-start(bf16[8,256,256]{2,1,0:T(8,128)(2,1)} %param.6) | copy-start | bytes 3145732
  7.2 59.8 %all-reduce.6.cloned.1.call-start = ((), (), s32[]{:S(2)}) async-start(), calls=%async_computation.2 | async-start | bytes 262144 | tf_op jit(solution)/shard_map/psum | solution.py:11
  24.6 88.4 %all-reduce.8.cloned.1.call-start = ((), (), s32[]{:S(2)}) async-start(), calls=%async_computation.3 | async-start | bytes 524288 | tf_op jit(solution)/shard_map/psum | solution.py:50
  25.3 0.7 copy-start.9
  27.1 0.7 copy-start.10
  29.1 0.7 copy-start.4
  29.8 113.5 %reduce-scatter.3.cloned.1.call-start = ((), (), s32[]{:S(2)}) async-start(), calls=%async_computation.4 | async-start | bytes 589824 | tf_op jit(solution)/shard_map/reduce_scatter | solution.py:55
  114.1 0.8 copy-start.2
  114.1 0.9 copy-start.8
  114.1 29.3 %copy-start.5 = (f32[128,128]{1,0:T(8,128)S(1)}, f32[128,128]{1,0:T(8,128)}, u32[]{:S(2)}) copy-start(f32[128,128]{1,0:T(8,128)} %param.11) | copy-start | bytes 196612
  114.9 88.2 %all-reduce.10.cloned.1.call-start = ((), (), s32[]{:S(2)}) async-start(), calls=%async_computation.5 | async-start | bytes 262144 | tf_op jit(solution)/shard_map/psum | solution.py:11
  163.6 85.2 %all-reduce.12.cloned.1.call-start = ((), (), s32[]{:S(2)}) async-start(), calls=%async_computation.6 | async-start | bytes 524288 | tf_op jit(solution)/shard_map/psum | solution.py:50
  165.8 0.7 copy-start.3
  166.5 112.4 %reduce-scatter.5.cloned.1.call-start = ((), (), s32[]{:S(2)}) async-start(), calls=%async_computation.7 | async-start | bytes 589824 | tf_op jit(solution)/shard_map/reduce_scatter | solution.py:55
  249.9 0.8 copy-start.1
  249.9 29.1 %copy-start.7 = (f32[128,128]{1,0:T(8,128)S(1)}, f32[128,128]{1,0:T(8,128)}, u32[]{:S(2)}) copy-start(f32[128,128]{1,0:T(8,128)} %reduce-scatter.3.cloned.1.call-done) | copy-start | bytes 196612
  250.7 155.4 %all-reduce.14.cloned.1.call-start = ((), (), s32[]{:S(2)}) async-start(), calls=%async_computation.8 | async-start | bytes 131072 | tf_op jit(solution)/shard_map/psum | solution.py:68
  279.8 0.9 copy-start.6
Sparse Core Ops, SparseCore 0:
  24.8 42.1 all-reduce.5
  70.1 42.8 all-reduce.7
  115.3 28.0 reduce-scatter.2
  163.7 39.3 all-reduce.9
  205.9 42.9 all-reduce.11
  251.0 27.8 reduce-scatter.4
  285.1 120.9 all-reduce.13
where the time goes:
time: 415 us; the launch traced here: 414 us
  waiting for transfers between devices  332 us (80%)
  blocking collectives  33.8 us (8%)
  between operations  17.7 us (4%)
  local copies, waits for them, and re-layouts  12.8 us (3%)
  other arithmetic  12.8 us (3%)
  matrix products  5.15 us (1%)
    psum x1, waiting for transfers between devices, on_device(): gram_total = lax.psum(gram_local, ('row', 'col'))  125 us
    psum x2, waiting for transfers between devices, apply_hamiltonian(): column_total = lax.psum(col_part, 'row')  79.5 us
    psum x2, waiting for transfers between devices, spread(): return lax.psum(block, axis)  73.6 us
    reduce_scatter x2, waiting for transfers between devices, apply_hamiltonian(): return lax.psum_scatter(row_part, 'col', scatter_dimension=0, tiled=True)  53.5 us
    all_gather x2, blocking collectives, apply_hamiltonian(): row_panel = lax.all_gather(vector_panel, 'col', axis=0, tiled=True)  33.8 us
  transfers between devices with their start and end apart: 7, of which 7 were waited for; matrix products, arithmetic and copies ran while one was open for 4% of the time, Pallas kernels for 0%

commit v1 on v0

--- a/solution.py
+++ b/solution.py
@@ -2,6 +2,7 @@
 import jax.numpy as jnp
 from jax import lax
 from jax.sharding import PartitionSpec as P
+from jax.lax import axis_size, ppermute
 
 BLK_COL = 2
 
@@ -47,7 +48,13 @@
         )
         row_part = start_rows.at[tile_rows].add(forward)
         col_part = start_cols.at[tile_cols].add(backward)
-        column_total = lax.psum(col_part, "row")
+        nd = axis_size("row")
+        column_total = col_part
+        for no in [
+            [(ii, ii ^ src_i) for ii in range(nd)] for src_i in (1, 2, 4, 8, 16) if src_i < nd
+        ]:
+            res = ppermute(column_total, "row", no)
+            column_total = column_total + res
         row_part = row_part.reshape(group_rows, width_vecs)
         present = lax.dynamic_slice_in_dim(row_part, offset, column_rows, 0)
         updated = present + owner_flag * column_total.reshape(column_rows, width_vecs)

time: 415 us -> 346 us (0.83)
  waiting for transfers between devices: 332 us -> 262 us
  starting transfers between devices: 0.29 us -> 5.1 us
    psum x2 -> x0, waiting for transfers between devices: 79.5 us -> none  [apply_hamiltonian(): column_total = lax.psum(col_part, 'row')]
    psum x2, waiting for transfers between devices: 73.6 us -> 80.3 us  [spread(): return lax.psum(block, axis)]
    ppermute x0 -> x4, starting transfers between devices: none -> 4.89 us  [apply_hamiltonian(): res = ppermute(column_total, 'row', no)]
  transfers between devices with their start and end apart: 7 -> 9, of which waited for: 7 -> 7; matrix products, arithmetic and copies ran while one was open for 4% -> 4% of each run, Pallas kernels for 0% -> 0%
where the time goes in v1:
time: 346 us
  waiting for transfers between devices  262 us (76%)
  blocking collectives  33.9 us (10%)
  between operations  17.3 us (5%)
  other arithmetic  11.6 us (3%)
  local copies, waits for them, and re-layouts  10.8 us (3%)
  matrix products  5.13 us (1%)
  starting transfers between devices  5.1 us (1%)
    psum x1, waiting for transfers between devices, on_device(): gram_total = lax.psum(gram_local, ('row', 'col'))  125 us
    psum x2, waiting for transfers between devices, spread(): return lax.psum(block, axis)  80.3 us
    reduce_scatter x2, waiting for transfers between devices, apply_hamiltonian(): return lax.psum_scatter(row_part, 'col', scatter_dimension=0, tiled=True)  54.5 us
    all_gather x2, blocking collectives, apply_hamiltonian(): row_panel = lax.all_gather(vector_panel, 'col', axis=0, tiled=True)  33.9 us
  transfers between devices with their start and end apart: 9, of which 7 were waited for; matrix products, arithmetic and copies ran while one was open for 4% of the time, Pallas kernels for 0%

profile of v1, /device:TPU:1, one launch (start us, length us, event | category | flops | bytes accessed | tf_op | source)
XLA Modules:
  0.0 346.0 jit_solution(2220492196004717446)
XLA Ops:
  7.2 0.7 compare_select_fusion.1
  8.0 0.8 convert_element_type.16
  8.8 15.8 %all_gather.6 = bf16[1024,128]{1,0:T(8,128)(2,1)S(1)} all-gather(bf16[128,128]{1,0:T(8,128)(2,1)S(1)} %convert_element_type.16), channel_id=1, replica_groups=mesh['row'=4,'col'=8] {'col'}, dimensions={0}, use_global_device_ids=true | all-gather | bytes 294912 | tf_op jit(solution)/shard_map/all_gather | solution.py:36
  27.0 1.3 scatter_fusion.1
  28.3 1.3 collective-permute-start
  29.6 0.7 dynamic-slice_select_fusion.1
  30.4 41.6 %all-reduce.4.cloned.1.call-done = bf16[2,256,128]{2,1,0:T(8,128)(2,1)} async-done(((bf16[2,256,128]{2,1,0:T(8,128)(2,1)}), bf16[2,256,128]{2,1,0:T(8,128)(2,1)}) %all-reduce.4.cloned.1.call-update) | async-done | bytes 131088 | tf_op jit(solution)/shard_map/psum | solution.py:12
  72.0 1.5 gather_fusion
  73.6 1.1 collective-permute-start.1
  74.7 1.7 convolution_bitcast_fusion.3
  76.4 1.5 copy.13
  78.0 1.3 scatter_fusion
  79.4 1.0 collective-permute-done.1
  80.5 0.8 copy-done.2
  84.5 25.7 %reduce-scatter.3.cloned.1.call-done = f32[128,128]{1,0:T(8,128)} async-done(((f32[1024,128]{1,0:T(8,128)}), f32[128,128]{1,0:T(8,128)}) %reduce-scatter.3.cloned.1.call-update) | async-done | bytes 65552 | tf_op jit(solution)/shard_map/reduce_scatter | solution.py:62
  110.2 0.9 fusion.8
  111.1 18.2 %all_gather.7 = bf16[1024,128]{1,0:T(8,128)(2,1)S(1)} all-gather(bf16[128,128]{1,0:T(8,128)(2,1)S(1)} %fusion.8), channel_id=1, replica_groups=mesh['row'=4,'col'=8] {'col'}, dimensions={0}, use_global_device_ids=true | all-gather | bytes 294912 | tf_op jit(solution)/shard_map/all_gather | solution.py:36
  130.7 1.3 scatter_fusion.3
  132.0 1.3 collective-permute-start.2
  134.1 38.7 %all-reduce.6.cloned.1.call-done = bf16[2,256,128]{2,1,0:T(8,128)(2,1)} async-done(((bf16[2,256,128]{2,1,0:T(8,128)(2,1)}), bf16[2,256,128]{2,1,0:T(8,128)(2,1)}) %all-reduce.6.cloned.1.call-update) | async-done | bytes 131088 | tf_op jit(solution)/shard_map/psum | solution.py:12
  172.8 1.5 gather_fusion.2
  174.4 1.1 collective-permute-start.3
  175.6 1.7 convolution_bitcast_fusion.1
  177.3 1.5 copy.17
  178.9 1.3 scatter_fusion.2
  180.2 1.0 collective-permute-done.3
  181.3 0.8 copy-done.1
  182.2 28.9 %reduce-scatter.5.cloned.1.call-done = f32[128,128]{1,0:T(8,128)} async-done(((f32[1024,128]{1,0:T(8,128)}), f32[128,128]{1,0:T(8,128)}) %reduce-scatter.5.cloned.1.call-update) | async-done | bytes 65552 | tf_op jit(solution)/shard_map/reduce_scatter | solution.py:62
  211.0 0.9 divide_subtract_fusion
  211.9 0.9 fusion.10
  212.9 125.1 %all-reduce.8.cloned.1.call-done = f32[128,128]{1,0:T(8,128)} async-done(((f32[128,128]{1,0:T(8,128)}), f32[128,128]{1,0:T(8,128)}) %all-reduce.8.cloned.1.call-update) | async-done | bytes 65552 | tf_op jit(solution)/shard_map/psum | solution.py:75
  338.0 1.5 broadcast_multiply_fusion
  (56 shorter events, 5.1 us)
Async XLA Ops:
  7.2 18.7 %copy-start = (bf16[8,256,256]{2,1,0:T(8,128)(2,1)S(1)}, bf16[8,256,256]{2,1,0:T(8,128)(2,1)}, u32[]{:S(2)}) copy-start(bf16[8,256,256]{2,1,0:T(8,128)(2,1)} %param.6) | copy-start | bytes 3145732
  7.2 64.8 %all-reduce.4.cloned.1.call-start = ((), (), s32[]{:S(2)}) async-start(), calls=%async_computation.2 | async-start | bytes 262144 | tf_op jit(solution)/shard_map/psum | solution.py:12
  24.6 1.3 copy-start.3
  26.3 0.7 copy-start.11
  27.0 2.6 copy-start.4
  28.3 45.2 %collective-permute-start = (f32[2,256,128]{2,1,0:T(8,128)S(1)}, f32[2,256,128]{2,1,0:T(8,128)S(1)}, u32[]{:S(2)}, u32[]{:S(2)}) collective-permute-start(f32[2,256,128]{2,1,0:T(8,128)S(1)} %scatter_fusion.1), channel_id=1, source_target_pairs={{0,8},{8,0},{16,24},{24,16},{1,9},{9,1},{17,25},{25,17},{2,10},{10... | collective-permute-start | bytes 786440 | tf_op jit(solution)/shard_map/ppermute | solution.py:56
  30.3 79.9 %reduce-scatter.3.cloned.1.call-start = ((), (), s32[]{:S(2)}) async-start(), calls=%async_computation.3 | async-start | bytes 589824 | tf_op jit(solution)/shard_map/reduce_scatter | solution.py:62
  73.6 6.8 %collective-permute-start.1 = (f32[2,256,128]{2,1,0:T(8,128)S(1)}, f32[2,256,128]{2,1,0:T(8,128)S(1)}, u32[]{:S(2)}, u32[]{:S(2)}) collective-permute-start(f32[2,256,128]{2,1,0:T(8,128)S(1)} %add.69), channel_id=1, source_target_pairs={{0,16},{8,24},{16,0},{24,8},{1,17},{9,25},{17,1},{25,9},{2,18},{10... | collective-permute-start | bytes 786440 | tf_op jit(solution)/shard_map/ppermute | solution.py:56
  80.5 0.8 copy-start.2
  80.5 0.9 copy-start.10
  80.5 29.7 %copy-start.7 = (f32[128,128]{1,0:T(8,128)S(1)}, f32[128,128]{1,0:T(8,128)}, u32[]{:S(2)}) copy-start(f32[128,128]{1,0:T(8,128)} %param.11) | copy-start | bytes 196612
  81.3 91.5 %all-reduce.6.cloned.1.call-start = ((), (), s32[]{:S(2)}) async-start(), calls=%async_computation.4 | async-start | bytes 262144 | tf_op jit(solution)/shard_map/psum | solution.py:12
  129.2 0.7 copy-start.5
  130.7 2.7 copy-start.6
  132.0 42.3 %collective-permute-start.2 = (f32[2,256,128]{2,1,0:T(8,128)S(1)}, f32[2,256,128]{2,1,0:T(8,128)S(1)}, u32[]{:S(2)}, u32[]{:S(2)}) collective-permute-start(f32[2,256,128]{2,1,0:T(8,128)S(1)} %scatter_fusion.3), channel_id=1, source_target_pairs={{0,8},{8,0},{16,24},{24,16},{1,9},{9,1},{17,25},{25,17},{2,10},{10... | collective-permute-start | bytes 786440 | tf_op jit(solution)/shard_map/ppermute | solution.py:56
  134.1 76.9 %reduce-scatter.5.cloned.1.call-start = ((), (), s32[]{:S(2)}) async-start(), calls=%async_computation.5 | async-start | bytes 589824 | tf_op jit(solution)/shard_map/reduce_scatter | solution.py:62
  174.4 6.8 %collective-permute-start.3 = (f32[2,256,128]{2,1,0:T(8,128)S(1)}, f32[2,256,128]{2,1,0:T(8,128)S(1)}, u32[]{:S(2)}, u32[]{:S(2)}) collective-permute-start(f32[2,256,128]{2,1,0:T(8,128)S(1)} %add.73), channel_id=1, source_target_pairs={{0,16},{8,24},{16,0},{24,8},{1,17},{9,25},{17,1},{25,9},{2,18},{10... | collective-permute-start | bytes 786440 | tf_op jit(solution)/shard_map/ppermute | solution.py:56
  181.3 0.8 copy-start.1
  181.3 29.7 %copy-start.9 = (f32[128,128]{1,0:T(8,128)S(1)}, f32[128,128]{1,0:T(8,128)}, u32[]{:S(2)}) copy-start(f32[128,128]{1,0:T(8,128)} %reduce-scatter.3.cloned.1.call-done) | copy-start | bytes 196612
  182.1 155.8 %all-reduce.8.cloned.1.call-start = ((), (), s32[]{:S(2)}) async-start(), calls=%async_computation.6 | async-start | bytes 131072 | tf_op jit(solution)/shard_map/psum | solution.py:75
  211.9 0.9 copy-start.8
Sparse Core Ops, SparseCore 0:
  30.5 41.4 all-reduce.3
  81.4 28.7 reduce-scatter.2
  134.2 38.5 all-reduce.5
  182.2 28.7 reduce-scatter.4
  217.0 120.8 all-reduce.7
